TPU v7x, 32 devices: a whole 2x2x4 slice. The times are simulated.
32 devices in a mesh: groups: 2 (over x), tile: 8 (over z, y), ex: 2 (over core).
Axes of the slice: x: 2, y: 2, z: 4, core: 2. Of those that a mesh axis runs over, the one named last changes fastest.
Arguments:
- train_in: bfloat16 [256, 32, 8192], P(('groups', 'ex'), None, 'tile'), parts along dimension 0, may hold values from -6 to 6
- train_out: bfloat16 [256, 32, 28672], P(('groups', 'ex'), None, 'tile'), parts along dimension 0, may hold values from -6 to 6
- query_in: bfloat16 [128, 32, 8192], P(('groups', 'ex'), None, 'tile'), parts along dimension 0, may hold values from -6 to 6
- query_out: bfloat16 [128, 32, 28672], P(('groups', 'ex'), None, 'tile'), parts along dimension 0, may hold values from -6 to 6
- basis_in: bfloat16 [8192, 512], P('tile'), may hold values from -0.0625 to 0.0625
- basis_out: bfloat16 [28672, 2048], P('tile'), may hold values from -0.046875 to 0.046875
- eigenvalues: float32 [512, 2048], P(None, 'tile'), may hold values from 0.1 to 10
Outputs:
- scores: float32 [64, 256], P('tile', ('groups', 'ex')), parts along dimension 1
There are 2 independent parts, one for each index of `groups`. A program takes and returns all parts, laid end to end along the dimension named above; an argument that names none is the same for every part. Nothing has to cross between parts.
All inputs are finite; a program needn't handle non-finite values.
Results may differ from a plain program's by a relative error of at most 0.025.
Values may be sent and summed in bfloat16 or wider, within the bound.
A program may use at most 192 MiB of HBM per device.

v0:
```python
import math

import jax
import jax.numpy as jnp
from jax import lax
from jax.sharding import PartitionSpec as P

damping = 0.1


def on_device(train_in, train_out, query_in, query_out, basis_in, basis_out, eigenvalues):
    train_count, rank_width, in_part = train_in.shape
    query_count = query_in.shape[0]
    out_part = train_out.shape[2]
    width_in = basis_in.shape[1]
    width_out = basis_out.shape[1]
    tile_count = lax.axis_size("tile")
    local_out = width_out // tile_count
    in_rows = jnp.concatenate(
        [train_in.reshape(-1, in_part), query_in.reshape(-1, in_part)], axis=0
    )
    out_rows = jnp.concatenate(
        [train_out.reshape(-1, out_part), query_out.reshape(-1, out_part)], axis=0
    )
    partial_in = jnp.dot(in_rows, basis_in, preferred_element_type=jnp.float32)
    rot_in = lax.psum(partial_in.astype(jnp.bfloat16), "tile")
    rot_out = lax.psum_scatter(
        lax.dot_general(
            basis_out, out_rows, (((0,), (1,)), ((), ())), preferred_element_type=jnp.float32
        ).astype(jnp.bfloat16),
        "tile",
        scatter_dimension=0,
        tiled=True,
    )
    train_rows = train_count * rank_width
    train_rin = rot_in[:train_rows].reshape(train_count, rank_width, width_in)
    query_rin = rot_in[train_rows:].reshape(query_count, rank_width, width_in)
    train_rout = rot_out[:, :train_rows].reshape(local_out, train_count, rank_width)
    query_rout = rot_out[:, train_rows:].reshape(local_out, query_count, rank_width)
    train_rot = jnp.einsum(
        "nri,jnr->nij", train_rin, train_rout, preferred_element_type=jnp.float32
    ).astype(jnp.bfloat16)
    inverse = 1.0 / (eigenvalues + damping)
    local_weighted = (
        jnp.einsum("mri,jmr->mij", query_rin, query_rout, preferred_element_type=jnp.float32)
        * inverse
    ).astype(jnp.bfloat16)
    weighted = lax.all_gather(local_weighted, "ex", axis=0, tiled=True)
    every_query = weighted.shape[0]
    partial_scores = lax.dot_general(
        weighted.reshape(every_query, -1),
        train_rot.reshape(train_count, -1),
        (((1,), (1,)), ((), ())),
        preferred_element_type=jnp.float32,
    )
    summed = lax.psum_scatter(partial_scores, "tile", scatter_dimension=0, tiled=True)
    factor = 1.0 / (rank_width * math.sqrt(width_in * width_out))
    return summed * factor


def solution(mesh):
    return jax.shard_map(
        on_device,
        mesh=mesh,
        in_specs=(
            P(("groups", "ex"), None, "tile"),
            P(("groups", "ex"), None, "tile"),
            P(("groups", "ex"), None, "tile"),
            P(("groups", "ex"), None, "tile"),
            P("tile", None),
            P("tile", None),
            P(None, "tile"),
        ),
        out_specs=P("tile", ("groups", "ex")),
        check_vma=False,
    )
```

profile of v0, /device:TPU:0, one launch (start us, length us, event | category | flops | bytes accessed | tf_op | source)
XLA Modules:
  0.0 478.1 jit_solution(3653401042907661946)
XLA Ops:
  6.5 0.0 copy-start
  6.5 0.0 all-reduce.3.cloned.1.call-start
  6.5 1.2 copy-done
  7.8 7.9 %fusion.12 = bf16[3072,512]{1,0:T(8,128)(2,1)} fusion(bf16[1024,512]{1,0:T(8,128)(2,1)S(1)} %copy-done, bf16[1024,1024]{1,0:T(8,128)(2,1)} %bitcast.29, bf16[2048,1024]{1,0:T(8,128)(2,1)} %bitcast.28), kind=kOutput, calls=%fused_computation.13 | convolution fusion | flops 3235381248 | bytes 10485760 | tf_op jit(solution)/shard_map/dot_general | solution.py:25
  15.7 0.0 all-reduce.3.cloned.1.call-update
  15.7 0.0 reduce-scatter.2.cloned.1.call-start
  15.7 0.0 copy-start.3
  15.7 54.4 %convert_bitcast_fusion = bf16[2048,3072]{0,1:T(8,128)(2,1)} fusion(bf16[3584,2048]{1,0:T(8,128)(2,1)} %param.12, bf16[1024,3584]{1,0:T(8,128)(2,1)} %bitcast.27, bf16[2048,3584]{1,0:T(8,128)(2,1)} %bitcast.26), kind=kOutput, calls=%fused_computation.8 | convolution fusion | flops 45147488256 | bytes 49283072 | tf_op jit(solution)/shard_map/dot_general | solution.py:28
  70.1 0.0 reduce-scatter.2.cloned.1.call-update
  70.2 0.2 all-gather.2.cloned.1.call-start
  70.4 0.0 copy-done.3
  70.4 0.9 add_divide_fusion
  71.3 76.1 %all-reduce.3.cloned.1.call-done = bf16[3072,512]{1,0:T(8,128)(2,1)} async-done(((bf16[3072,512]{1,0:T(8,128)(2,1)}), bf16[3072,512]{1,0:T(8,128)(2,1)}) %all-reduce.3.cloned.1.call-update) | async-done | bytes 3145744 | tf_op jit(solution)/shard_map/psum | solution.py:26
  147.4 1.3 slice.16
  148.7 209.4 %reduce-scatter.2.cloned.1.call-done = bf16[256,3072]{0,1:T(8,128)(2,1)} async-done(((bf16[2048,3072]{0,1:T(8,128)(2,1)}), bf16[256,3072]{0,1:T(8,128)(2,1)}) %reduce-scatter.2.cloned.1.call-update) | async-done | bytes 1572880 | tf_op jit(solution)/shard_map/reduce_scatter | solution.py:27
  358.0 1.1 slice.17
  359.2 2.4 fusion.18
  361.6 0.0 copy-done.2
  361.6 0.0 copy-start.4
  361.6 0.0 slice-start
  361.6 17.3 %fusion.5 = bf16[32,512,256]{2,0,1:T(8,128)(2,1)} fusion(f32[32,512,256]{2,1,0:T(8,128)S(1)} %fusion.18, f32[512,256]{1,0:T(8,128)S(1)} %copy-done.2), kind=kLoop, calls=%fused_computation.7 | loop fusion | flops 8388608 | bytes 25690112 | tf_op jit(solution)/shard_map/convert_element_type | solution.py:47
  378.9 0.0 all-gather.2.cloned.1.call-update
  379.0 0.0 copy-done.4
  379.0 0.6 dynamic-slice
  380.2 2.3 slice.19
  382.5 0.0 slice-done
  382.5 13.5 %fusion.19 = bf16[64,512,256]{2,1,0:T(8,128)(2,1)} fusion(bf16[64,32,512]{2,1,0:T(8,128)(2,1)S(1)} %bitcast.22, bf16[256,64,32]{0,2,1:T(8,128)(2,1)} %bitcast.24), kind=kOutput, calls=%fused_computation.20 | convolution fusion | flops 536870912 | bytes 19922944 | tf_op jit(solution)/shard_map/nri,jnr->nij/dot_general | solution.py:40
  396.0 12.4 %all-gather.2.cloned.1.call-done = bf16[64,512,256]{2,0,1:T(8,128)(2,1)} async-done(((bf16[32,512,256]{2,0,1:T(8,128)(2,1)}), bf16[64,512,256]{2,0,1:T(8,128)(2,1)}) %all-gather.2.cloned.1.call-update) | async-done | bytes 16777232 | tf_op jit(solution)/shard_map/all_gather | solution.py:48
  408.3 25.3 %fusion.15 = f32[64,64]{1,0:T(8,128)S(1)} fusion(bf16[64,512,256]{2,0,1:T(8,128)(2,1)} %all-gather.2.cloned.1.call-done, bf16[64,512,256]{2,1,0:T(8,128)(2,1)} %fusion.19), kind=kOutput, calls=%fused_computation.14 | convolution fusion | flops 1073741824 | bytes 33570816 | tf_op jit(solution)/shard_map/dot_general | solution.py:50
  433.6 37.4 %all-reduce = f32[64,64]{1,0:T(8,128)S(1)} all-reduce(f32[64,64]{1,0:T(8,128)S(1)} %fusion.15), channel_id=3, replica_groups=mesh['groups'=2,'tile'=8,'ex'=2] {'tile'}, use_global_device_ids=true, to_apply=%region_2.0.clone | all-reduce | flops 4096 | bytes 32768
  470.9 0.6 dynamic-slice_multiply_fusion
  471.5 0.0 copy-done.1
  (2 shorter events, 0.0 us)
Async XLA Ops:
  6.5 1.2 copy-start
  6.5 140.8 %all-reduce.3.cloned.1.call-start = ((), (), s32[]{:S(2)}) async-start(), calls=%async_computation.1 | async-start | bytes 6291456 | tf_op jit(solution)/shard_map/psum | solution.py:26
  15.7 342.4 %reduce-scatter.2.cloned.1.call-start = ((), (), s32[]{:S(2)}) async-start(), calls=%async_computation.2 | async-start | bytes 14155776 | tf_op jit(solution)/shard_map/reduce_scatter | solution.py:27
  15.7 54.7 %copy-start.3 = (f32[512,256]{1,0:T(8,128)S(1)}, f32[512,256]{1,0:T(8,128)}, u32[]{:S(2)}) copy-start(f32[512,256]{1,0:T(8,128)} %param.13) | copy-start | bytes 1572868
  70.2 338.2 %all-gather.2.cloned.1.call-start = ((), (), s32[]{:S(2)}) async-start(), calls=%async_computation.3 | async-start | bytes 25165824 | tf_op jit(solution)/shard_map/all_gather | solution.py:48
  358.0 3.5 copy-start.2
  361.6 17.4 %copy-start.4 = (u32[32]{0:T(128)S(1)}, u32[32]{0:T(128)}, u32[]{:S(2)}) copy-start(u32[32]{0:T(128)} %constant.8) | copy-start | bytes 388
  361.6 20.9 %slice-start = ((bf16[3072,512]{1,0:T(8,128)(2,1)}), bf16[2048,512]{1,0:T(8,128)(2,1)S(1)}, s32[]{:S(2)}) async-start(bf16[3072,512]{1,0:T(8,128)(2,1)} %all-reduce.3.cloned.1.call-done), calls=%async_computation.4 | async-start | bytes 4194304 | tf_op jit(solution)/shard_map/slice | solution.py:36
  382.5 89.1 %copy-start.1 = (bf16[1024,512]{1,0:T(8,128)(2,1)S(1)}, bf16[1024,512]{1,0:T(8,128)(2,1)}, u32[]{:S(2)}) copy-start(bf16[1024,512]{1,0:T(8,128)(2,1)} %param.11) | copy-start | bytes 3145732
Sparse Core Ops, SparseCore 0:
  15.8 131.5 all-reduce.2
  151.4 206.5 reduce-scatter.1
  379.1 29.1 all-gather.1
where the time goes:
time: 478 us
  waiting for transfers between devices  298 us (62%)
  matrix products  103 us (22%)
  blocking collectives  37.4 us (8%)
  other arithmetic  18.8 us (4%)
  between operations  13.8 us (3%)
  local copies, waits for them, and re-layouts  6.51 us (1%)
    reduce_scatter x1, waiting for transfers between devices, on_device(): lax.psum_scatter(lax.dot_general(basis_out, out_rows, (((0,), (1,)), ((),...  209 us
    psum x1, waiting for transfers between devices, on_device(): rot_in = lax.psum(partial_in.astype(jnp.bfloat16), 'tile')  76.1 us
    dot_general x1, matrix products, on_device(): lax.dot_general(basis_out, out_rows, (((0,), (1,)), ((), ())), preferred_...  54.4 us
    unnamed x1, blocking collectives  37.4 us
    dot_general x1, matrix products, on_device(): lax.dot_general(weighted.reshape(every_query, -1), train_rot.reshape(trai...  25.3 us
    convert_element_type x1, other arithmetic, on_device(): local_weighted = (jnp.einsum('mri,jmr->mij', query_rin, query_rout, prefe...  17.3 us
    dot_general x1, matrix products, on_device(): jnp.einsum('nri,jnr->nij', train_rin, train_rout, preferred_element_type=...  13.5 us
    all_gather x1, waiting for transfers between devices, on_device(): weighted = lax.all_gather(local_weighted, 'ex', axis=0, tiled=True)  12.4 us
  transfers between devices with their start and end apart: 3, of which 3 were waited for; matrix products, arithmetic and copies ran while one was open for 15% of the time, Pallas kernels for 0%

commit v1 on v0

v1 whole, which is shorter than its diff:
```python
import functools
import math

import jax
import jax.numpy as jnp
from jax import lax
from jax.experimental import pallas as pl
from jax.experimental.pallas import tpu as pltpu
from jax.sharding import PartitionSpec as P

damping = 0.1
MESH = pl.DeviceIdType.MESH
SUBS = 2


def tile_at(place, tiles, snake):
    if not snake:
        return place
    return jnp.where(place < tiles // 2, 2 * place, 2 * (tiles - 1 - place) + 1)


def place_of(tile, tiles, snake):
    if not snake:
        return tile
    return jnp.where(tile % 2 == 0, tile // 2, tiles - 1 - tile // 2)


def rotate_kernel(tiles, snake, train_in, train_out, query_in, query_out, basis_in, basis_out,
                  train_rin, train_rout, query_rin, query_rout,
                  rows_in, rows_out, basis_in_v, basis_v, slots, slots_in, rin,
                  load_sem, basis_sem, send_sem, recv_sem, send_in, recv_in, store_sem, ex_send, ex_recv):
    me = place_of(lax.axis_index("tile"), tiles, snake)
    ex = lax.axis_index("ex")
    right = tile_at((me + 1) % tiles, tiles, snake)
    left = tile_at((me + tiles - 1) % tiles, tiles, snake)
    toward = (right, left)
    train_rows, query_rows = train_in.shape[0], query_in.shape[0]
    rows = train_rows + query_rows
    width = slots.shape[-1]
    item = rows // (2 * SUBS)
    chunk = rows // tiles
    half = chunk // 2

    def target(way, step):
        if way == 0:
            return (me + 2 * tiles - 1 - step) % tiles
        return (me + 1 + step) % tiles

    def load(source, dest, n):
        return pltpu.make_async_copy(source, dest, load_sem.at[n])

    loads = [
        load(basis_in, basis_in_v, 0),
        load(train_in, rows_in.at[pl.ds(0, train_rows)], 1),
        load(query_in, rows_in.at[pl.ds(train_rows, query_rows)], 2),
        load(train_out, rows_out.at[pl.ds(0, train_rows)], 3),
        load(query_out, rows_out.at[pl.ds(train_rows, query_rows)], 4),
    ]

    def basis_copy(way, step):
        column = pl.multiple_of(tile_at(target(way, step), tiles, snake) * width, width)
        return pltpu.make_async_copy(
            basis_out.at[:, pl.ds(column, width)], basis_v.at[way, step % 2], basis_sem.at[way, step % 2]
        )

    for copy in loads[:3]:
        copy.start()
    for way in range(2):
        basis_copy(way, 0).start()
    for copy in loads[3:]:
        copy.start()

    barrier = pltpu.get_barrier_semaphore()
    for neighbour in toward:
        pl.semaphore_signal(barrier, inc=1, device_id={"tile": neighbour}, device_id_type=MESH)
    pl.semaphore_signal(barrier, inc=1, device_id={"ex": 1 - ex}, device_id_type=MESH)
    pl.semaphore_wait(barrier, 3)

    def send(way, sub, step):
        return pltpu.make_async_remote_copy(
            src_ref=slots.at[way, sub, step], dst_ref=slots.at[way, sub, step + 1],
            send_sem=send_sem.at[way, sub, step], recv_sem=recv_sem.at[way, sub, step + 1],
            device_id={"tile": toward[way]}, device_id_type=MESH,
        )

    def arrived(way, sub, step):
        return pltpu.make_async_remote_copy(
            src_ref=slots.at[way, sub, step], dst_ref=slots.at[way, sub, step],
            send_sem=send_sem.at[way, sub, step], recv_sem=recv_sem.at[way, sub, step],
            device_id={"tile": toward[way]}, device_id_type=MESH,
        )

    def out_step(way, sub, step):
        start = (way * SUBS + sub) * item
        product = jnp.dot(
            rows_out[pl.ds(start, item), :], basis_v[way, step % 2], preferred_element_type=jnp.float32
        )

        @pl.when(step == 0)
        def _():
            slots[way, sub, 0] = product.astype(jnp.bfloat16)

        @pl.when(step > 0)
        def _():
            arrived(way, sub, step).wait_recv()
            slots[way, sub, step] = (product + slots[way, sub, step].astype(jnp.float32)).astype(jnp.bfloat16)

        @pl.when(step < tiles - 1)
        def _():
            send(way, sub, step).start()

    def span(way, place):
        return pl.ds(pl.multiple_of(place * chunk + way * half, half), half)

    def hop_in(way, k, source, dest):
        return pltpu.make_async_remote_copy(
            src_ref=source, dst_ref=dest, send_sem=send_in.at[way, k], recv_sem=recv_in.at[way, k + 1],
            device_id={"tile": toward[way]}, device_id_type=MESH,
        )

    def in_sum(way, k):
        product = jnp.dot(
            rows_in[span(way, target(way, k)), :], basis_in_v[...], preferred_element_type=jnp.float32
        )

        @pl.when(k == 0)
        def _():
            slots_in[way, 0] = product.astype(jnp.bfloat16)

        @pl.when(k > 0)
        def _():
            hop_in(way, k - 1, slots_in.at[way, k], slots_in.at[way, k]).wait_recv()
            slots_in[way, k] = (product + slots_in[way, k].astype(jnp.float32)).astype(jnp.bfloat16)

        @pl.when(k < tiles - 1)
        def _():
            hop_in(way, k, slots_in.at[way, k], slots_in.at[way, k + 1]).start()

        @pl.when(k == tiles - 1)
        def _():
            rin[span(way, me), :] = slots_in[way, tiles - 1]
            piece = rin.at[span(way, me)]
            hop_in(way, k, piece, piece).start()

    def in_spread(way, k):
        hops = k - (tiles - 1)
        place = (me + tiles - hops) % tiles if way == 0 else (me + hops) % tiles
        piece = rin.at[span(way, place)]

        @pl.when(k < 2 * tiles - 1)
        def _():
            hop_in(way, k - 1, piece, piece).wait_recv()

        @pl.when(k < 2 * tiles - 2)
        def _():
            hop_in(way, k, piece, piece).start()

    def in_step(k):
        @pl.when(k < tiles)
        def _():
            for way in range(2):
                in_sum(way, k)

        @pl.when(k >= tiles)
        def _():
            for way in range(2):
                in_spread(way, k)

    for copy in loads[:3]:
        copy.wait()

    def step_body(step, carry):
        in_step(2 * step)

        @pl.when(step == 0)
        def _():
            for copy in loads[3:]:
                copy.wait()

        for way in range(2):
            basis_copy(way, step).wait()

        @pl.when(step < tiles - 1)
        def _():
            for way in range(2):
                basis_copy(way, step + 1).start()

        for sub in range(SUBS):
            if sub == SUBS // 2:
                in_step(2 * step + 1)
            for way in range(2):
                out_step(way, sub, step)
        return carry

    lax.fori_loop(0, tiles, step_body, 0)

    stores = []
    exchanges = []

    def store(source, dest):
        copy = pltpu.make_async_copy(source, dest, store_sem.at[len(stores)])
        copy.start()
        stores.append(copy)

    def exchange(source, dest):
        n = len(exchanges)
        copy = pltpu.make_async_remote_copy(
            src_ref=source, dst_ref=dest, send_sem=ex_send.at[n], recv_sem=ex_recv.at[n],
            device_id={"ex": 1 - ex}, device_id_type=MESH,
        )
        copy.start()
        exchanges.append(copy)

    base = pl.multiple_of(ex * query_rows, query_rows)
    query_piece = rin.at[pl.ds(train_rows, query_rows)]
    exchange(query_piece, query_rin.at[pl.ds(base, query_rows)])
    store(query_piece, query_rin.at[pl.ds(base, query_rows)])
    store(rin.at[pl.ds(0, train_rows)], train_rin)
    for i in range(2 * SUBS):
        low, high = i * item, (i + 1) * item
        held = slots.at[i // SUBS, i % SUBS, tiles - 1]
        cut = min(max(train_rows, low), high)
        if cut < high:
            offset = pl.multiple_of(base + (cut - train_rows), 16)
            dest = query_rout.at[pl.ds(offset, high - cut)]
            exchange(held.at[pl.ds(cut - low, high - cut)], dest)
            store(held.at[pl.ds(cut - low, high - cut)], dest)
        if low < cut:
            store(held.at[pl.ds(0, cut - low)], train_rout.at[pl.ds(low, cut - low)])

    def finish(step, carry):
        for way in range(2):
            for sub in range(SUBS):
                send(way, sub, step).wait_send()
        return carry

    lax.fori_loop(0, tiles - 1, finish, 0)

    def finish_in(k, carry):
        for way in range(2):
            piece = slots_in.at[way, 0]
            hop_in(way, k, piece, piece).wait_send()
        return carry

    lax.fori_loop(0, 2 * tiles - 2, finish_in, 0)
    for copy in exchanges:
        copy.wait()
    for copy in stores:
        copy.wait()


def rotate(tiles, snake, train_in, train_out, query_in, query_out, basis_in, basis_out):
    train_rows, in_part = train_in.shape
    query_rows, out_part = query_out.shape
    rows = train_rows + query_rows
    ka = basis_in.shape[1]
    width = basis_out.shape[1] // tiles
    item = rows // (2 * SUBS)
    half = rows // tiles // 2
    dtype = jnp.bfloat16
    flops = 2 * rows * (in_part * ka + out_part * basis_out.shape[1])
    return pl.pallas_call(
        functools.partial(rotate_kernel, tiles, snake),
        out_shape=(
            jax.ShapeDtypeStruct((train_rows, ka), dtype),
            jax.ShapeDtypeStruct((train_rows, width), dtype),
            jax.ShapeDtypeStruct((2 * query_rows, ka), dtype),
            jax.ShapeDtypeStruct((2 * query_rows, width), dtype),
        ),
        in_specs=[pl.BlockSpec(memory_space=pl.ANY)] * 6,
        out_specs=(pl.BlockSpec(memory_space=pl.ANY),) * 4,
        scratch_shapes=[
            pltpu.VMEM((rows, in_part), dtype),
            pltpu.VMEM((rows, out_part), dtype),
            pltpu.VMEM((in_part, ka), dtype),
            pltpu.VMEM((2, 2, out_part, width), dtype),
            pltpu.VMEM((2, SUBS, tiles, item, width), dtype),
            pltpu.VMEM((2, tiles, half, ka), dtype),
            pltpu.VMEM((rows, ka), dtype),
            pltpu.SemaphoreType.DMA((5,)),
            pltpu.SemaphoreType.DMA((2, 2)),
            pltpu.SemaphoreType.DMA((2, SUBS, tiles)),
            pltpu.SemaphoreType.DMA((2, SUBS, tiles)),
            pltpu.SemaphoreType.DMA((2, 2 * tiles)),
            pltpu.SemaphoreType.DMA((2, 2 * tiles)),
            pltpu.SemaphoreType.DMA((2 * SUBS + 4,)),
            pltpu.SemaphoreType.DMA((2 * SUBS + 1,)),
            pltpu.SemaphoreType.DMA((2 * SUBS + 1,)),
        ],
        compiler_params=pltpu.CompilerParams(
            collective_id=0, has_side_effects=True, vmem_limit_bytes=60 * 1024 * 1024
        ),
        cost_estimate=pl.CostEstimate(flops=flops, bytes_accessed=50_000_000, transcendentals=0),
        name="rotate",
    )(train_in, train_out, query_in, query_out, basis_in, basis_out)


def sum_kernel(tiles, factor, part, out, landed, send_sem, recv_sem):
    me = lax.axis_index("tile")
    barrier = pltpu.get_barrier_semaphore()
    for d in range(1, tiles):
        pl.semaphore_signal(barrier, inc=1, device_id={"tile": (me + d) % tiles}, device_id_type=MESH)
    pl.semaphore_wait(barrier, tiles - 1)
    copies = []
    for d in range(1, tiles):
        to = (me + d) % tiles
        copy = pltpu.make_async_remote_copy(
            src_ref=part.at[to], dst_ref=landed.at[d], send_sem=send_sem.at[d], recv_sem=recv_sem.at[d],
            device_id={"tile": to}, device_id_type=MESH,
        )
        copy.start()
        copies.append(copy)
    total = part[me]
    for d in range(1, tiles):
        copies[d - 1].wait_recv()
        total = total + landed[d]
    out[...] = total * factor
    for copy in copies:
        copy.wait_send()


def sum_scores(tiles, factor, part):
    return pl.pallas_call(
        functools.partial(sum_kernel, tiles, factor),
        out_shape=jax.ShapeDtypeStruct(part.shape[1:], jnp.float32),
        in_specs=[pl.BlockSpec(memory_space=pltpu.VMEM)],
        out_specs=pl.BlockSpec(memory_space=pltpu.VMEM),
        scratch_shapes=[
            pltpu.VMEM(part.shape, jnp.float32),
            pltpu.SemaphoreType.DMA((tiles,)),
            pltpu.SemaphoreType.DMA((tiles,)),
        ],
        compiler_params=pltpu.CompilerParams(collective_id=1, has_side_effects=True),
        name="sum_scores",
    )(part)


def on_device(snake, train_in, train_out, query_in, query_out, basis_in, basis_out, eigenvalues):
    train_count, rank_width, in_part = train_in.shape
    query_count = query_in.shape[0]
    out_part = train_out.shape[2]
    width_in = basis_in.shape[1]
    width_out = basis_out.shape[1]
    tiles = lax.axis_size("tile")
    local_out = width_out // tiles
    every_query = 2 * query_count
    train_rin, train_rout, query_rin, query_rout = rotate(
        tiles, snake,
        train_in.reshape(-1, in_part), train_out.reshape(-1, out_part),
        query_in.reshape(-1, in_part), query_out.reshape(-1, out_part), basis_in, basis_out,
    )
    train_rin = train_rin.reshape(train_count, rank_width, width_in)
    query_rin = query_rin.reshape(every_query, rank_width, width_in)
    train_rout = train_rout.reshape(train_count, rank_width, local_out)
    query_rout = query_rout.reshape(every_query, rank_width, local_out)
    train_rot = jnp.einsum(
        "nri,nrj->nij", train_rin, train_rout, preferred_element_type=jnp.float32
    ).astype(jnp.bfloat16)
    inverse = 1.0 / (eigenvalues + damping)
    weighted = (
        jnp.einsum("mri,mrj->mij", query_rin, query_rout, preferred_element_type=jnp.float32) * inverse
    ).astype(jnp.bfloat16)
    partial_scores = lax.dot_general(
        weighted, train_rot, (((1, 2), (1, 2)), ((), ())), preferred_element_type=jnp.float32
    )
    factor = 1.0 / (rank_width * math.sqrt(width_in * width_out))
    return sum_scores(tiles, factor, partial_scores.reshape(tiles, every_query // tiles, train_count))


def solution(mesh):
    snake = mesh.shape["tile"] == 8
    return jax.shard_map(
        functools.partial(on_device, snake),
        mesh=mesh,
        in_specs=(
            P(("groups", "ex"), None, "tile"),
            P(("groups", "ex"), None, "tile"),
            P(("groups", "ex"), None, "tile"),
            P(("groups", "ex"), None, "tile"),
            P("tile", None),
            P("tile", None),
            P(None, "tile"),
        ),
        out_specs=P("tile", ("groups", "ex")),
        check_vma=False,
    )
```

time: 478 us -> 279 us (0.58)
  waiting for transfers between devices: 298 us -> 0 us
  Pallas kernels: 0 us -> 211 us
  blocking collectives: 37.4 us -> 0 us
  matrix products: 103 us -> 65.9 us
  other arithmetic: 18.8 us -> 1.12 us
  between operations: 13.8 us -> 0.04 us
  local copies, waits for them, and re-layouts: 6.51 us -> 1.28 us
    pallas_call x0 -> x2, Pallas kernels: none -> 211 us  [the longest x1 202 us: rotate(): pl.pallas_call(functools.partial(rotate_kernel, tiles, snake), out_shape=...]
    reduce_scatter x1 -> x0, waiting for transfers between devices: 209 us -> none  [on_device(): lax.psum_scatter(lax.dot_general(basis_out, out_rows, (((0,), (1,)), ((),...]
    psum x1 -> x0, waiting for transfers between devices: 76.1 us -> none  [on_device(): rot_in = lax.psum(partial_in.astype(jnp.bfloat16), 'tile')]
    dot_general x5 -> x3, matrix products: 103 us -> 65.9 us  [the longest x1 40.2 us: on_device(): lax.dot_general(weighted, train_rot, (((1, 2), (1, 2)), ((), ())), prefer...]
    unnamed x1 -> x0, blocking collectives: 37.4 us -> none
    convert_element_type x1 -> x0, other arithmetic: 17.3 us -> none  [on_device(): local_weighted = (jnp.einsum('mri,jmr->mij', query_rin, query_rout, prefe...]
    all_gather x1 -> x0, waiting for transfers between devices: 12.4 us -> none  [on_device(): weighted = lax.all_gather(local_weighted, 'ex', axis=0, tiled=True)]
  transfers between devices with their start and end apart: 3 -> 0, of which waited for: 3 -> 0; matrix products, arithmetic and copies ran while one was open for 15% -> 0% of each run, Pallas kernels for 0% -> 0%
where the time goes in v1:
time: 279 us
  Pallas kernels  211 us (76%)
  matrix products  65.9 us (24%)
    pallas_call x1, Pallas kernels, rotate(): pl.pallas_call(functools.partial(rotate_kernel, tiles, snake), out_shape=...  202 us
    dot_general x1, matrix products, on_device(): lax.dot_general(weighted, train_rot, (((1, 2), (1, 2)), ((), ())), prefer...  40.2 us
    dot_general x1, matrix products, on_device(): jnp.einsum('mri,mrj->mij', query_rin, query_rout, preferred_element_type=...  17.6 us
    pallas_call x1, Pallas kernels, sum_scores(): pl.pallas_call(functools.partial(sum_kernel, tiles, factor), out_shape=ja...  8.28 us
    dot_general x1, matrix products, on_device(): jnp.einsum('nri,nrj->nij', train_rin, train_rout, preferred_element_type=...  8.09 us

profile of v1, /device:TPU:0, one launch (start us, length us, event | category | flops | bytes accessed | tf_op | source)
XLA Modules:
  0.0 278.9 jit_solution(11217251910604801109)
XLA Ops:
  0.0 202.2 %rotate.1 = (bf16[2048,512]{1,0:T(8,128)(2,1)}, bf16[2048,256]{1,0:T(8,128)(2,1)}, bf16[2048,512]{1,0:T(8,128)(2,1)}, bf16[2048,256]{1,0:T(8,128)(2,1)}) custom-call(bf16[2048,1024]{1,0:T(8,128)(2,1)} %bitcast.22, bf16[2048,3584]{1,0:T(8,128)(2,1)} %bitcast.20, bf16[1024,1024]{1,0:T(8,128)(2,1)} %bitcast.23, bf16[1024,3584]{1,0:T(8,128)(2,1)} %bitcast.21, ...), custom_call_target="tpu_custom_call" | custom-call | flops 48318382080 | bytes 50000000 | tf_op jit(solution)/shard_map/rotate/pallas_call | solution.py:262
  202.3 0.0 copy-start
  202.3 0.0 copy-start.1
  202.3 17.6 %fusion.7 = f32[64,512,256]{2,1,0:T(8,128)} fusion(bf16[64,32,512]{2,1,0:T(8,128)(2,1)} %bitcast.17, bf16[64,32,256]{2,1,0:T(8,128)(2,1)} %bitcast.19), kind=kOutput, calls=%fused_computation.7 | convolution fusion | flops 536870912 | bytes 36700160 | tf_op jit(solution)/shard_map/mri,mrj->mij/dot_general | solution.py:361
  219.9 0.0 copy-done
  219.9 0.0 copy-done.1
  219.9 8.1 %fusion.8 = bf16[64,512,256]{2,1,0:T(8,128)(2,1)} fusion(bf16[64,32,512]{2,1,0:T(8,128)(2,1)S(1)} %bitcast.16, bf16[64,32,256]{2,1,0:T(8,128)(2,1)S(1)} %bitcast.18), kind=kOutput, calls=%fused_computation.8 | convolution fusion | flops 536870912 | bytes 19922944 | tf_op jit(solution)/shard_map/nri,nrj->nij/dot_general | solution.py:356
  228.0 1.1 add_divide_fusion
  229.1 40.2 %fusion.4.part = f32[8,8,64]{2,1,0:T(8,128)} fusion(bf16[64,512,256]{2,1,0:T(8,128)(2,1)} %fusion.8, f32[64,512,256]{2,1,0:T(8,128)} %fusion.7, f32[512,256]{1,0:T(8,128)S(1)} %add_divide_fusion), kind=kOutput, calls=%fused_computation.5 | convolution fusion | flops 1090519040 | bytes 50872320 | tf_op jit(solution)/shard_map/dot_general | solution.py:363
  269.3 8.3 %sum_scores.1 = f32[8,64]{1,0:T(8,128)} custom-call(f32[8,8,64]{2,1,0:T(8,128)} %fusion.4.part), custom_call_target="tpu_custom_call" | custom-call | tf_op jit(solution)/shard_map/sum_scores/pallas_call | solution.py:323
  277.6 1.3 copy.21
Async XLA Ops:
  202.3 17.6 %copy-start = (bf16[2048,512]{1,0:T(8,128)(2,1)S(1)}, bf16[2048,512]{1,0:T(8,128)(2,1)}, u32[]{:S(2)}) copy-start(bf16[2048,512]{1,0:T(8,128)(2,1)} %get-tuple-element.11) | copy-start | bytes 6291460
  202.3 17.6 %copy-start.1 = (bf16[2048,256]{1,0:T(8,128)(2,1)S(1)}, bf16[2048,256]{1,0:T(8,128)(2,1)}, u32[]{:S(2)}) copy-start(bf16[2048,256]{1,0:T(8,128)(2,1)} %get-tuple-element.12) | copy-start | bytes 3145732

commit v2 on v1

--- a/solution.py
+++ b/solution.py
@@ -10,7 +10,7 @@
 
 damping = 0.1
 MESH = pl.DeviceIdType.MESH
-SUBS = 2
+SUBS = 4
 
 
 def tile_at(place, tiles, snake):

time: 279 us -> 278 us (level)
  no operation moved by 1% of the time
where the time goes in v2:
time: 278 us; the launch traced here: 277 us
  Pallas kernels  209 us (75%)
  matrix products  65.9 us (24%)
    pallas_call x1, Pallas kernels, rotate(): pl.pallas_call(functools.partial(rotate_kernel, tiles, snake), out_shape=...  201 us
    dot_general x1, matrix products, on_device(): lax.dot_general(weighted, train_rot, (((1, 2), (1, 2)), ((), ())), prefer...  40.2 us
    dot_general x1, matrix products, on_device(): jnp.einsum('mri,mrj->mij', query_rin, query_rout, preferred_element_type=...  17.6 us
    pallas_call x1, Pallas kernels, sum_scores(): pl.pallas_call(functools.partial(sum_kernel, tiles, factor), out_shape=ja...  8.28 us
    dot_general x1, matrix products, on_device(): jnp.einsum('nri,nrj->nij', train_rin, train_rout, preferred_element_type=...  8.09 us

profile of v2, /device:TPU:0, one launch (start us, length us, event | category | flops | bytes accessed | tf_op | source)
XLA Modules:
  0.0 277.3 jit_solution(8535940707845932131)
XLA Ops:
  0.0 200.7 %rotate.1 = (bf16[2048,512]{1,0:T(8,128)(2,1)}, bf16[2048,256]{1,0:T(8,128)(2,1)}, bf16[2048,512]{1,0:T(8,128)(2,1)}, bf16[2048,256]{1,0:T(8,128)(2,1)}) custom-call(bf16[2048,1024]{1,0:T(8,128)(2,1)} %bitcast.22, bf16[2048,3584]{1,0:T(8,128)(2,1)} %bitcast.20, bf16[1024,1024]{1,0:T(8,128)(2,1)} %bitcast.23, bf16[1024,3584]{1,0:T(8,128)(2,1)} %bitcast.21, ...), custom_call_target="tpu_custom_call" | custom-call | flops 48318382080 | bytes 50000000 | tf_op jit(solution)/shard_map/rotate/pallas_call | solution.py:262
  200.7 0.0 copy-start
  200.7 0.0 copy-start.1
  200.7 17.6 %fusion.7 = f32[64,512,256]{2,1,0:T(8,128)} fusion(bf16[64,32,512]{2,1,0:T(8,128)(2,1)} %bitcast.17, bf16[64,32,256]{2,1,0:T(8,128)(2,1)} %bitcast.19), kind=kOutput, calls=%fused_computation.7 | convolution fusion | flops 536870912 | bytes 36700160 | tf_op jit(solution)/shard_map/mri,mrj->mij/dot_general | solution.py:361
  218.3 0.0 copy-done
  218.3 0.0 copy-done.1
  218.3 8.1 %fusion.8 = bf16[64,512,256]{2,1,0:T(8,128)(2,1)} fusion(bf16[64,32,512]{2,1,0:T(8,128)(2,1)S(1)} %bitcast.16, bf16[64,32,256]{2,1,0:T(8,128)(2,1)S(1)} %bitcast.18), kind=kOutput, calls=%fused_computation.8 | convolution fusion | flops 536870912 | bytes 19922944 | tf_op jit(solution)/shard_map/nri,nrj->nij/dot_general | solution.py:356
  226.4 1.1 add_divide_fusion
  227.5 40.2 %fusion.4.part = f32[8,8,64]{2,1,0:T(8,128)} fusion(bf16[64,512,256]{2,1,0:T(8,128)(2,1)} %fusion.8, f32[64,512,256]{2,1,0:T(8,128)} %fusion.7, f32[512,256]{1,0:T(8,128)S(1)} %add_divide_fusion), kind=kOutput, calls=%fused_computation.5 | convolution fusion | flops 1090519040 | bytes 50872320 | tf_op jit(solution)/shard_map/dot_general | solution.py:363
  267.7 8.3 %sum_scores.1 = f32[8,64]{1,0:T(8,128)} custom-call(f32[8,8,64]{2,1,0:T(8,128)} %fusion.4.part), custom_call_target="tpu_custom_call" | custom-call | tf_op jit(solution)/shard_map/sum_scores/pallas_call | solution.py:323
  276.0 1.3 copy.21
Async XLA Ops:
  200.7 17.6 %copy-start = (bf16[2048,512]{1,0:T(8,128)(2,1)S(1)}, bf16[2048,512]{1,0:T(8,128)(2,1)}, u32[]{:S(2)}) copy-start(bf16[2048,512]{1,0:T(8,128)(2,1)} %get-tuple-element.11) | copy-start | bytes 6291460
  200.7 17.6 %copy-start.1 = (bf16[2048,256]{1,0:T(8,128)(2,1)S(1)}, bf16[2048,256]{1,0:T(8,128)(2,1)}, u32[]{:S(2)}) copy-start(bf16[2048,256]{1,0:T(8,128)(2,1)} %get-tuple-element.12) | copy-start | bytes 3145732
